TPU v7x, 32 devices: a whole 2x2x4 slice. The times are simulated.
32 devices in a mesh: hours: 2 (over x), lon: 8 (over z, y), lat: 2 (over core).
Axes of the slice: x: 2, y: 2, z: 4, core: 2. Of those that a mesh axis runs over, the one named last changes fastest.
Arguments:
- field: float32 [16, 512, 2048], P('hours', 'lon', 'lat'), parts along dimension 0, may hold values from -6 to 6
- longitude_matrix: float32 [1024, 512], P(('hours', 'lon')), parts along dimension 0, may hold values from -0.25 to 0.25
- latitude_matrix: float32 [4096, 256], P(('hours', 'lat')), parts along dimension 0, may hold values from -0.125 to 0.125
Outputs:
- core: float32 [16, 512, 256], P('hours', 'lon', 'lat'), parts along dimension 0
There are 2 independent parts, one for each index of `hours`. A program takes and returns all parts, laid end to end along the dimension named above; each array names one. Nothing has to cross between parts.
All inputs are finite; a program needn't handle non-finite values.
Results may differ from a plain program's by a relative error of at most 0.000073.
Values sent between devices are 32-bit elements; how exact they have to be, the bound alone decides.
A program may use at most 64 MiB of HBM per device.

v0:
```python
import jax
import jax.numpy as jnp
from jax import lax
from jax.sharding import PartitionSpec as P


def body(field, longitude_matrix, latitude_matrix):
    highest_precision = lax.Precision.HIGHEST
    columns = latitude_matrix
    reduced_core = lax.psum_scatter(
        jnp.einsum("mb,vnm->bvn", columns, field, precision=highest_precision),
        "lat",
        scatter_dimension=0,
        tiled=True,
    )
    columns = longitude_matrix
    collected_parts = lax.psum_scatter(
        jnp.einsum("bvn,na->avb", reduced_core, columns, precision=highest_precision),
        "lon",
        scatter_dimension=0,
        tiled=True,
    )
    core = jnp.transpose(collected_parts, (1, 0, 2))
    return core


def solution(mesh):
    in_specs = (P("hours", "lon", "lat"), P(("hours", "lon"), None), P(("hours", "lat"), None))
    out_specs = P("hours", "lon", "lat")
    return jax.shard_map(body, mesh=mesh, in_specs=in_specs, out_specs=out_specs, check_vma=False)
```

profile of v0, /device:TPU:0, one launch (start us, length us, event | category | flops | bytes accessed | tf_op | source)
XLA Modules:
  0.0 107.4 jit_solution(17552693487201788414)
XLA Ops:
  6.5 0.0 copy-start
  6.5 0.0 copy-start.1
  6.5 0.0 reduce-scatter.3.cloned.1.call-start
  6.5 1.6 %copy-done = f32[8,64,1024]{2,1,0:T(8,128)S(1)} copy-done((f32[8,64,1024]{2,1,0:T(8,128)S(1)}, f32[8,64,1024]{2,1,0:T(8,128)}, u32[]{:S(2)}) %copy-start) | copy-done | bytes 2097176
  8.1 3.9 %fusion = f32[256,8,64]{0,2,1:T(8,128)} fusion(f32[8,64,1024]{2,1,0:T(8,128)S(1)} %copy-done, f32[1024,256]{1,0:T(8,128)} %param.5), kind=kOutput, calls=%fused_computation.1 | convolution fusion | flops 1610612736 | bytes 3670016 | tf_op jit(solution)/shard_map/mb,vnm->bvn/dot_general | solution.py:11
  12.0 0.0 reduce-scatter.3.cloned.1.call-update
  12.0 0.0 reduce-scatter.5.cloned.1.call-start
  12.1 10.7 %reduce-scatter.3.cloned.1.call-done = f32[128,8,64]{0,2,1:T(8,128)} async-done(((f32[256,8,64]{0,2,1:T(8,128)}), f32[128,8,64]{0,2,1:T(8,128)}) %reduce-scatter.3.cloned.1.call-update) | async-done | bytes 262160 | tf_op jit(solution)/shard_map/reduce_scatter | solution.py:10
  22.8 0.0 copy-done.1
  22.8 4.1 %convolution_bitcast_fusion = f32[512,8,128]{0,2,1:T(8,128)} fusion(f32[128,8,64]{0,2,1:T(8,128)} %reduce-scatter.3.cloned.1.call-done, f32[64,512]{1,0:T(8,128)S(1)} %copy-done.1), kind=kOutput, calls=%fused_computation | convolution fusion | flops 402653184 | bytes 2490368 | tf_op jit(solution)/shard_map/bvn,na->avb/dot_general | solution.py:18
  26.9 2.9 %copy.5 = f32[512,8,128]{2,1,0:T(8,128)} copy(f32[512,8,128]{0,2,1:T(8,128)} %convolution_bitcast_fusion) | data formatting | bytes 4194304 | tf_op jit(solution)/shard_map/bvn,na->avb/transpose | solution.py:18
  29.8 0.0 reduce-scatter.5.cloned.1.call-update
  29.9 69.0 %reduce-scatter.5.cloned.1.call-done = f32[64,8,128]{2,1,0:T(8,128)} async-done(((f32[512,8,128]{2,1,0:T(8,128)}), f32[64,8,128]{2,1,0:T(8,128)}) %reduce-scatter.5.cloned.1.call-update) | async-done | bytes 262160 | tf_op jit(solution)/shard_map/reduce_scatter | solution.py:17
  98.8 1.7 %copy.6 = f32[8,64,128]{2,1,0:T(8,128)} copy(f32[8,64,128]{2,0,1:T(8,128)} %bitcast.11) | data formatting | bytes 524288 | tf_op jit(solution)/shard_map/transpose | solution.py:23
Async XLA Ops:
  6.5 1.6 %copy-start = (f32[8,64,1024]{2,1,0:T(8,128)S(1)}, f32[8,64,1024]{2,1,0:T(8,128)}, u32[]{:S(2)}) copy-start(f32[8,64,1024]{2,1,0:T(8,128)} %param.3) | copy-start | bytes 6291460
  6.5 16.3 %copy-start.1 = (f32[64,512]{1,0:T(8,128)S(1)}, f32[64,512]{1,0:T(8,128)}, u32[]{:S(2)}) copy-start(f32[64,512]{1,0:T(8,128)} %param.4) | copy-start | bytes 393220
  6.5 16.3 %reduce-scatter.3.cloned.1.call-start = ((), (), s32[]{:S(2)}) async-start(), calls=%async_computation.2 | async-start | bytes 786432 | tf_op jit(solution)/shard_map/reduce_scatter | solution.py:10
  12.0 86.8 %reduce-scatter.5.cloned.1.call-start = ((), (), s32[]{:S(2)}) async-start(), calls=%async_computation.3 | async-start | bytes 2359296 | tf_op jit(solution)/shard_map/reduce_scatter | solution.py:17
Sparse Core Ops, SparseCore 0:
  12.1 10.6 reduce-scatter.2
  30.0 68.8 reduce-scatter.4
where the time goes:
time: 108 us; the launch traced here: 107 us
  waiting for transfers between devices  79.7 us (74%)
  between operations  13.4 us (12%)
  matrix products  7.99 us (7%)
  local copies, waits for them, and re-layouts  6.19 us (6%)
    reduce_scatter x1, waiting for transfers between devices, body(): lax.psum_scatter(jnp.einsum('bvn,na->avb', reduced_core, columns, precisi...  69 us
    reduce_scatter x1, waiting for transfers between devices, body(): lax.psum_scatter(jnp.einsum('mb,vnm->bvn', columns, field, precision=high...  10.7 us
    dot_general x1, matrix products, body(): jnp.einsum('bvn,na->avb', reduced_core, columns, precision=highest_precis...  4.13 us
    dot_general x1, matrix products, body(): jnp.einsum('mb,vnm->bvn', columns, field, precision=highest_precision)  3.86 us
    transpose x1, local copies, waits for them, and re-layouts, body(): jnp.einsum('bvn,na->avb', reduced_core, columns, precision=highest_precis...  2.89 us
  transfers between devices with their start and end apart: 2, of which 2 were waited for; matrix products, arithmetic and copies ran while one was open for 0% of the time, Pallas kernels for 0%

commit v1 on v0

v1 whole, which is shorter than its diff:
```python
import functools

import jax
import jax.numpy as jnp
from jax import lax
from jax.experimental import pallas as pl
from jax.experimental.pallas import tpu as pltpu
from jax.sharding import PartitionSpec as P

F32 = jnp.float32
BF16 = jnp.bfloat16


def split(x):
    hi = x.astype(BF16)
    return hi, (x - hi.astype(F32)).astype(BF16)


def dot(a, b):
    return jnp.dot(a, b, preferred_element_type=F32)


def kernel(
    chunks, y_size,
    field_hbm, lon_hbm, lat_hbm, out_ref,
    field_buf, lat_buf, lon_buf, lat_hi, lat_lo, lon_hi, lon_lo,
    mine, sent, got, level_buf, core_buf,
    field_sem, lat_sem, lon_sem, pair_send, pair_recv,
    lon_send, lon_recv, share_send, share_recv,
    one_send, one_recv, two_send, two_recv,
):
    levels, rows, depth = field_buf.shape
    width = mine.shape[2]
    peers = levels
    half = rows // 2
    z_size = peers // y_size
    per = levels // chunks
    me = lax.axis_index("lon")
    core = lax.axis_index("lat")
    other = 1 - core
    z, y = me // y_size, lax.rem(me, y_size)

    def remote(src, dst, send_sem, recv_sem, target):
        return pltpu.make_async_remote_copy(
            src_ref=src, dst_ref=dst, send_sem=send_sem, recv_sem=recv_sem,
            device_id=target, device_id_type=pl.DeviceIdType.MESH,
        )

    my_half = pl.ds(pl.multiple_of(core * half, half), half)
    lon_in = pltpu.make_async_copy(lon_hbm.at[my_half], lon_buf.at[me, my_half], lon_sem)
    lon_in.start()
    lat_in = []
    for part, who in ((0, core), (1, other)):
        columns = pl.ds(pl.multiple_of(who * width, width), width)
        copy = pltpu.make_async_copy(
            lat_hbm.at[:, columns], lat_buf.at[:, pl.ds(part * width, width)], lat_sem.at[part]
        )
        copy.start()
        lat_in.append(copy)
    field_in = []
    for c in range(chunks):
        span = pl.ds(c * per, per)
        copy = pltpu.make_async_copy(field_hbm.at[span], field_buf.at[span], field_sem.at[c])
        copy.start()
        field_in.append(copy)

    barrier = pltpu.get_barrier_semaphore()
    for d in range(1, peers):
        pl.semaphore_signal(
            barrier, inc=1, device_id={"lon": lax.rem(me + d, peers)}, device_id_type=pl.DeviceIdType.MESH
        )
    pl.semaphore_signal(barrier, inc=1, device_id={"lat": other}, device_id_type=pl.DeviceIdType.MESH)
    pl.semaphore_wait(barrier, peers)

    def lon_copy(shard, slot, target):
        ref = lon_buf.at[shard, my_half]
        return remote(ref, ref, lon_send.at[slot], lon_recv.at[shard], {"lon": target})

    mate = z * y_size + (1 - y)
    lon_in.wait()
    started = []
    for d in range(1, z_size):
        started.append(lon_copy(me, d - 1, lax.rem(z + d, z_size) * y_size + y))
    started.append(lon_copy(me, z_size - 1, mate))
    for copy in started:
        copy.start()

    for copy in lat_in:
        copy.wait()
    hi, lo = split(lat_buf[...])
    lat_hi[...] = hi
    lat_lo[...] = lo
    pair = []
    for c in range(chunks):
        field_in[c].wait()
        span = pl.ds(c * per, per)
        hi, lo = split(field_buf[span].reshape(per * rows, depth))
        total = dot(hi, lat_hi[...]) + dot(hi, lat_lo[...]) + dot(lo, lat_hi[...])
        sent[span] = total[:, width:].reshape(per, rows, width)
        copy = remote(sent.at[span], got.at[span], pair_send.at[c], pair_recv.at[c], {"lat": other})
        copy.start()
        pair.append(copy)
        mine[span] = total[:, :width].reshape(per, rows, width)

    def one_copy(level):
        return remote(mine.at[level], level_buf.at[me], one_send.at[level], one_recv.at[me], {"lon": level})

    for c in range(chunks):
        pair[c].wait_recv()
        span = pl.ds(c * per, per)
        mine[span] = mine[span] + got[span]
        for level in range(c * per, (c + 1) * per):
            @pl.when(me != level)
            def _():
                one_copy(level).start()

            @pl.when(me == level)
            def _():
                level_buf[level] = mine[level]

    def lon_arrived(shard):
        ref = lon_buf.at[shard, my_half]
        remote(ref, ref, lon_send.at[0], lon_recv.at[shard], {"lon": mate}).wait_recv()

    for d in range(1, z_size):
        shard = lax.rem(z + d, z_size) * y_size + y
        lon_arrived(shard)
        copy = lon_copy(shard, z_size - 1 + d, mate)
        copy.start()
        started.append(copy)
    for d in range(z_size):
        lon_arrived(lax.rem(z + d, z_size) * y_size + (1 - y))
    all_halves = lon_buf.at[:, my_half]
    share = remote(all_halves, all_halves, share_send, share_recv, {"lat": other})
    share.start()
    share.wait_recv()
    step = lon_hi.shape[1] // 4
    for block in range(lon_hi.shape[0] // step):
        cols = pl.ds(block * step, step)
        hi, lo = split(lon_buf[:, :, cols].reshape(peers * rows, step).T)
        lon_hi[cols] = hi
        lon_lo[cols] = lo

    for d in range(1, peers):
        source = lax.rem(me + d, peers)
        remote(mine.at[0], level_buf.at[source], one_send.at[0], one_recv.at[source], {"lon": source}).wait_recv()
    hi, lo = split(level_buf[...].reshape(peers * rows, width))
    core_buf[...] = (
        dot(lon_hi[...], hi) + dot(lon_hi[...], lo) + dot(lon_lo[...], hi)
    ).reshape(core_buf.shape)

    def two_copy(target):
        return remote(core_buf.at[target], out_ref.at[me], two_send.at[target], two_recv.at[me], {"lon": target})

    for d in range(1, peers):
        two_copy(lax.rem(me + d, peers)).start()
    out_ref[me] = core_buf[me]

    for copy in started:
        copy.wait_send()
    share.wait_send()
    for copy in pair:
        copy.wait_send()
    for d in range(1, peers):
        one_copy(lax.rem(me + d, peers)).wait_send()
    for d in range(1, peers):
        source = lax.rem(me + d, peers)
        remote(core_buf.at[0], out_ref.at[source], two_send.at[0], two_recv.at[source], {"lon": source}).wait_recv()
    for d in range(1, peers):
        two_copy(lax.rem(me + d, peers)).wait_send()


def exchanged(field, longitude_matrix, latitude_matrix):
    levels, rows, depth = field.shape
    rank = longitude_matrix.shape[1]
    columns = latitude_matrix.shape[1]
    peers = lax.axis_size("lon")
    width = columns // lax.axis_size("lat")
    block = rank // peers
    chunks, y_size = 2, 2
    z_size = peers // y_size
    dma = pltpu.SemaphoreType.DMA
    flops = 6 * (levels * rows * depth * columns + peers * rows * rank * width)
    return pl.pallas_call(
        functools.partial(kernel, chunks, y_size),
        out_shape=jax.ShapeDtypeStruct((levels, block, width), F32),
        in_specs=[pl.BlockSpec(memory_space=pltpu.HBM)] * 3,
        out_specs=pl.BlockSpec(memory_space=pltpu.VMEM),
        scratch_shapes=[
            pltpu.VMEM((levels, rows, depth), F32),
            pltpu.VMEM((depth, columns), F32),
            pltpu.VMEM((peers, rows, rank), F32),
            pltpu.VMEM((depth, columns), BF16),
            pltpu.VMEM((depth, columns), BF16),
            pltpu.VMEM((rank, peers * rows), BF16),
            pltpu.VMEM((rank, peers * rows), BF16),
            pltpu.VMEM((levels, rows, width), F32),
            pltpu.VMEM((levels, rows, width), F32),
            pltpu.VMEM((levels, rows, width), F32),
            pltpu.VMEM((peers, rows, width), F32),
            pltpu.VMEM((peers, block, width), F32),
            dma((chunks,)), dma((2,)), dma(()), dma((chunks,)), dma((chunks,)),
            dma((2 * z_size - 1,)), dma((peers,)), dma(()), dma(()),
            dma((peers,)), dma((peers,)), dma((peers,)), dma((peers,)),
        ],
        compiler_params=pltpu.CompilerParams(
            collective_id=0, has_side_effects=True, vmem_limit_bytes=40 * 1024 * 1024
        ),
        cost_estimate=pl.CostEstimate(
            flops=flops, bytes_accessed=4 * (field.size + longitude_matrix.size + latitude_matrix.size), transcendentals=0
        ),
    )(field, longitude_matrix, latitude_matrix)


def collected(field, longitude_matrix, latitude_matrix):
    highest = lax.Precision.HIGHEST
    reduced = lax.psum_scatter(
        jnp.einsum("mb,vnm->bvn", latitude_matrix, field, precision=highest),
        "lat", scatter_dimension=0, tiled=True,
    )
    parts = lax.psum_scatter(
        jnp.einsum("bvn,na->avb", reduced, longitude_matrix, precision=highest),
        "lon", scatter_dimension=0, tiled=True,
    )
    return jnp.transpose(parts, (1, 0, 2))


def body(field, longitude_matrix, latitude_matrix):
    if lax.axis_size("lat") == 2 and lax.axis_size("lon") == 8 == field.shape[0]:
        return exchanged(field, longitude_matrix, latitude_matrix)
    return collected(field, longitude_matrix, latitude_matrix)


def solution(mesh):
    in_specs = (P("hours", "lon", "lat"), P(("hours", "lon"), None), P(("hours", "lat"), None))
    out_specs = P("hours", "lon", "lat")
    return jax.shard_map(body, mesh=mesh, in_specs=in_specs, out_specs=out_specs, check_vma=False)
```

time: 108 us -> 33 us (0.31)
  the two profiles are of different devices: /device:TPU:0 before, /device:TPU:27 now
where the time goes in v1:
time: 33 us; the launch traced here: 32.8 us
  Pallas kernels  28.4 us (86%)
  local copies, waits for them, and re-layouts  4.42 us (13%)
    pallas_call x1, Pallas kernels, exchanged(): pl.pallas_call(functools.partial(kernel, chunks, y_size), out_shape=jax.S...  28.4 us
    unnamed x7, local copies, waits for them, and re-layouts  4.42 us

profile of v1, /device:TPU:27, one launch (start us, length us, event | category | flops | bytes accessed | tf_op | source)
XLA Modules:
  0.0 32.8 jit_solution(13507363415466384689)
XLA Ops:
  0.0 0.0 copy-start
  0.0 1.6 %copy-done = f32[8,64,1024]{2,1,0:T(8,128)S(1)} copy-done((f32[8,64,1024]{2,1,0:T(8,128)S(1)}, f32[8,64,1024]{2,1,0:T(8,128)}, u32[]{:S(2)}) %copy-start) | copy-done | bytes 2097176
  1.6 0.0 copy-start.1
  1.6 1.2 %copy-done.1 = f32[1024,256]{1,0:T(8,128)S(1)} copy-done((f32[1024,256]{1,0:T(8,128)S(1)}, f32[1024,256]{1,0:T(8,128)}, u32[]{:S(2)}) %copy-start.1) | copy-done | bytes 1048600
  2.8 0.0 copy-start.2
  2.8 0.9 %copy-done.2 = f32[64,512]{1,0:T(8,128)S(1)} copy-done((f32[64,512]{1,0:T(8,128)S(1)}, f32[64,512]{1,0:T(8,128)}, u32[]{:S(2)}) %copy-start.2) | copy-done | bytes 131096
  3.7 28.4 %shard_map.37 = f32[8,64,128]{2,1,0:T(8,128)S(1)} custom-call(f32[8,64,1024]{2,1,0:T(8,128)S(1)} %copy-done, f32[64,512]{1,0:T(8,128)S(1)} %copy-done.2, f32[1024,256]{1,0:T(8,128)S(1)} %copy-done.1), custom_call_target="tpu_custom_call" | custom-call | flops 1006632960 | bytes 3276800 | tf_op jit(solution)/shard_map/pallas_call | solution.py:184
  32.1 0.7 %copy.5 = f32[8,64,128]{2,1,0:T(8,128)} copy(f32[8,64,128]{2,1,0:T(8,128)S(1)} %shard_map.37) | data formatting | bytes 524288
Async XLA Ops:
  0.0 1.6 %copy-start = (f32[8,64,1024]{2,1,0:T(8,128)S(1)}, f32[8,64,1024]{2,1,0:T(8,128)}, u32[]{:S(2)}) copy-start(f32[8,64,1024]{2,1,0:T(8,128)} %field_hbm.1) | copy-start | bytes 6291460
  1.6 1.2 %copy-start.1 = (f32[1024,256]{1,0:T(8,128)S(1)}, f32[1024,256]{1,0:T(8,128)}, u32[]{:S(2)}) copy-start(f32[1024,256]{1,0:T(8,128)} %lat_hbm.1) | copy-start | bytes 3145732
  2.8 0.9 %copy-start.2 = (f32[64,512]{1,0:T(8,128)S(1)}, f32[64,512]{1,0:T(8,128)}, u32[]{:S(2)}) copy-start(f32[64,512]{1,0:T(8,128)} %lon_hbm.1) | copy-start | bytes 393220

commit v2 on v1

--- a/solution.py
+++ b/solution.py
@@ -40,6 +40,10 @@
     other = 1 - core
     z, y = me // y_size, lax.rem(me, y_size)
 
+    def flipped(along, across):
+        z_there = (z, z + 1 - 2 * lax.rem(z, 2), lax.rem(z + 2, z_size), z_size - 1 - z)[along]
+        return z_there, (y, 1 - y)[across]
+
     def remote(src, dst, send_sem, recv_sem, target):
         return pltpu.make_async_remote_copy(
             src_ref=src, dst_ref=dst, send_sem=send_sem, recv_sem=recv_sem,
@@ -77,57 +81,105 @@
         return remote(ref, ref, lon_send.at[slot], lon_recv.at[shard], {"lon": target})
 
     mate = z * y_size + (1 - y)
+    inner = (z == 1) | (z == 2)
+    first = 1 + lax.rem(z, 2)
+    second = jnp.where(lax.rem(z, 2) == 0, 2 + z // 2, z // 2)
+    outward = jnp.where(z == 1, 0, 3)
     lon_in.wait()
-    started = []
-    for d in range(1, z_size):
-        started.append(lon_copy(me, d - 1, lax.rem(z + d, z_size) * y_size + y))
-    started.append(lon_copy(me, z_size - 1, mate))
+    started = [
+        lon_copy(me, 0, first * y_size + y),
+        lon_copy(me, 1, second * y_size + y),
+        lon_copy(me, 2, mate),
+    ]
     for copy in started:
         copy.start()
+
+    def lon_arrived(shard):
+        ref = lon_buf.at[shard, my_half]
+        remote(ref, ref, lon_send.at[0], lon_recv.at[shard], {"lon": mate}).wait_recv()
+
+    def along_z(d):
+        return jnp.where(z < 2, lax.rem(z + d, z_size), lax.rem(z + z_size - d, z_size)) * y_size + y
+
+    def pass_copies(d, outwards):
+        shard = along_z(d)
+        copies = [lon_copy(shard, 2 + d, mate)]
+        if outwards:
+            copies.append(lon_copy(shard, 5 + d, outward * y_size + y))
+        return copies
+
+    def pass_on(d, outwards):
+        lon_arrived(along_z(d))
+        for copy in pass_copies(d, outwards):
+            copy.start()
 
     for copy in lat_in:
         copy.wait()
     hi, lo = split(lat_buf[...])
     lat_hi[...] = hi
     lat_lo[...] = lo
-    pair = []
-    for c in range(chunks):
+
+    def pair_copy(c):
+        span = pl.ds(c * per, per)
+        return remote(sent.at[span], got.at[span], pair_send.at[c], pair_recv.at[c], {"lat": other})
+
+    def contract(c):
         field_in[c].wait()
         span = pl.ds(c * per, per)
         hi, lo = split(field_buf[span].reshape(per * rows, depth))
         total = dot(hi, lat_hi[...]) + dot(hi, lat_lo[...]) + dot(lo, lat_hi[...])
         sent[span] = total[:, width:].reshape(per, rows, width)
-        copy = remote(sent.at[span], got.at[span], pair_send.at[c], pair_recv.at[c], {"lat": other})
-        copy.start()
-        pair.append(copy)
+        pair_copy(c).start()
         mine[span] = total[:, :width].reshape(per, rows, width)
 
-    def one_copy(level):
-        return remote(mine.at[level], level_buf.at[me], one_send.at[level], one_recv.at[me], {"lon": level})
-
-    for c in range(chunks):
-        pair[c].wait_recv()
+    def level_at(z_there, y_there):
+        return y_there * z_size + lax.rem(z_there, 2) * 2 + z_there // 2
+
+    my_level = level_at(z, y)
+
+    def one_copy(z_there, y_there):
+        return remote(
+            mine.at[level_at(z_there, y_there)], level_buf.at[me],
+            one_send.at[z_there * y_size + y_there], one_recv.at[me], {"lon": z_there * y_size + y_there},
+        )
+
+    def spread(c):
+        pair_copy(c).wait_recv()
         span = pl.ds(c * per, per)
         mine[span] = mine[span] + got[span]
-        for level in range(c * per, (c + 1) * per):
-            @pl.when(me != level)
-            def _():
-                one_copy(level).start()
-
-            @pl.when(me == level)
-            def _():
-                level_buf[level] = mine[level]
-
-    def lon_arrived(shard):
-        ref = lon_buf.at[shard, my_half]
-        remote(ref, ref, lon_send.at[0], lon_recv.at[shard], {"lon": mate}).wait_recv()
-
-    for d in range(1, z_size):
-        shard = lax.rem(z + d, z_size) * y_size + y
-        lon_arrived(shard)
-        copy = lon_copy(shard, z_size - 1 + d, mate)
-        copy.start()
-        started.append(copy)
+        for along in (3, 2, 1):
+            one_copy(flipped(along, 0)[0], c).start()
+
+        @pl.when(y != c)
+        def _():
+            one_copy(z, c).start()
+
+        @pl.when(y == c)
+        def _():
+            level_buf[me] = mine[my_level]
+
+    for c in range(chunks):
+        contract(c)
+        if c:
+            spread(c - 1)
+
+    @pl.when(inner)
+    def _():
+        pass_on(1, True)
+        pass_on(2, True)
+        pass_on(3, False)
+
+    @pl.when(~inner)
+    def _():
+        pass_on(1, False)
+
+    spread(chunks - 1)
+
+    @pl.when(~inner)
+    def _():
+        pass_on(2, False)
+        pass_on(3, False)
+
     for d in range(z_size):
         lon_arrived(lax.rem(z + d, z_size) * y_size + (1 - y))
     all_halves = lon_buf.at[:, my_half]
@@ -145,29 +197,46 @@
         source = lax.rem(me + d, peers)
         remote(mine.at[0], level_buf.at[source], one_send.at[0], one_recv.at[source], {"lon": source}).wait_recv()
     hi, lo = split(level_buf[...].reshape(peers * rows, width))
-    core_buf[...] = (
-        dot(lon_hi[...], hi) + dot(lon_hi[...], lo) + dot(lon_lo[...], hi)
-    ).reshape(core_buf.shape)
-
-    def two_copy(target):
-        return remote(core_buf.at[target], out_ref.at[me], two_send.at[target], two_recv.at[me], {"lon": target})
-
-    for d in range(1, peers):
-        two_copy(lax.rem(me + d, peers)).start()
-    out_ref[me] = core_buf[me]
+
+    def two_copy(z_there, y_there):
+        target = z_there * y_size + y_there
+        return remote(core_buf.at[target], out_ref.at[my_level], two_send.at[target], two_recv.at[me], {"lon": target})
+
+    block = core_buf.shape[1]
+    for along in (3, 2, 1, 0):
+        z_there, _ = flipped(along, 0)
+        cols = pl.ds(pl.multiple_of(z_there * y_size * block, y_size * block), y_size * block)
+        total = dot(lon_hi[cols], hi) + dot(lon_hi[cols], lo) + dot(lon_lo[cols], hi)
+        core_buf[pl.ds(z_there * y_size, y_size)] = total.reshape(y_size, block, width)
+        for across in (1, 0):
+            if along or across:
+                two_copy(*flipped(along, across)).start()
+    out_ref[my_level] = core_buf[me]
 
     for copy in started:
         copy.wait_send()
+    for d in range(1, z_size):
+        pass_copies(d, False)[0].wait_send()
+
+    @pl.when(inner)
+    def _():
+        for d in (1, 2):
+            pass_copies(d, True)[1].wait_send()
+
     share.wait_send()
-    for copy in pair:
-        copy.wait_send()
-    for d in range(1, peers):
-        one_copy(lax.rem(me + d, peers)).wait_send()
-    for d in range(1, peers):
-        source = lax.rem(me + d, peers)
-        remote(core_buf.at[0], out_ref.at[source], two_send.at[0], two_recv.at[source], {"lon": source}).wait_recv()
-    for d in range(1, peers):
-        two_copy(lax.rem(me + d, peers)).wait_send()
+    for c in range(chunks):
+        pair_copy(c).wait_send()
+    away = [(along, across) for along in range(z_size) for across in range(y_size) if along or across]
+    for place in away:
+        one_copy(*flipped(*place)).wait_send()
+    for place in away:
+        z_there, y_there = flipped(*place)
+        source = z_there * y_size + y_there
+        remote(
+            core_buf.at[0], out_ref.at[level_at(z_there, y_there)], two_send.at[0], two_recv.at[source], {"lon": source}
+        ).wait_recv()
+    for place in away:
+        two_copy(*flipped(*place)).wait_send()
 
 
 def exchanged(field, longitude_matrix, latitude_matrix):
@@ -200,11 +269,11 @@
             pltpu.VMEM((peers, rows, width), F32),
             pltpu.VMEM((peers, block, width), F32),
             dma((chunks,)), dma((2,)), dma(()), dma((chunks,)), dma((chunks,)),
-            dma((2 * z_size - 1,)), dma((peers,)), dma(()), dma(()),
+            dma((2 * z_size,)), dma((peers,)), dma(()), dma(()),
             dma((peers,)), dma((peers,)), dma((peers,)), dma((peers,)),
         ],
         compiler_params=pltpu.CompilerParams(
-            collective_id=0, has_side_effects=True, vmem_limit_bytes=40 * 1024 * 1024
+            collective_id=0, has_side_effects=True, vmem_limit_bytes=60 * 1024 * 1024
         ),
         cost_estimate=pl.CostEstimate(
             flops=flops, bytes_accessed=4 * (field.size + longitude_matrix.size + latitude_matrix.size), transcendentals=0

time: 33 us -> 28.6 us (0.87)
  the two profiles are of different devices: /device:TPU:27 before, /device:TPU:9 now
where the time goes in v2:
time: 28.6 us; the launch traced here: 28.5 us
  Pallas kernels  26.8 us (94%)
  local copies, waits for them, and re-layouts  1.67 us (6%)
    pallas_call x1, Pallas kernels, exchanged(): pl.pallas_call(functools.partial(kernel, chunks, y_size), out_shape=jax.S...  26.8 us
    unnamed x1, local copies, waits for them, and re-layouts  1.67 us

profile of v2, /device:TPU:9, one launch (start us, length us, event | category | flops | bytes accessed | tf_op | source)
XLA Modules:
  0.0 28.5 jit_solution(13193695604805367145)
XLA Ops:
  0.0 26.8 %shard_map.37 = f32[8,64,128]{2,1,0:T(8,128)} custom-call(f32[8,64,1024]{2,1,0:T(8,128)} %field_hbm.1, f32[64,512]{1,0:T(8,128)} %lon_hbm.1, f32[1024,256]{1,0:T(8,128)} %lat_hbm.1), custom_call_target="tpu_custom_call" | custom-call | flops 1006632960 | bytes 3276800 | tf_op jit(solution)/shard_map/pallas_call | solution.py:253
  26.8 1.7 %copy.5 = f32[8,64,128]{2,1,0:T(8,128)} copy(f32[8,64,128]{2,1,0:T(8,128)} %shard_map.37) | data formatting | bytes 524288

commit v3 on v2

--- a/solution.py
+++ b/solution.py
@@ -106,6 +106,7 @@
         copies = [lon_copy(shard, 2 + d, mate)]
         if outwards:
             copies.append(lon_copy(shard, 5 + d, outward * y_size + y))
+            copies.append(lon_copy(shard, 7 + d, outward * y_size + (1 - y)))
         return copies
 
     def pass_on(d, outwards):
@@ -160,8 +161,6 @@
 
     for c in range(chunks):
         contract(c)
-        if c:
-            spread(c - 1)
 
     @pl.when(inner)
     def _():
@@ -173,12 +172,14 @@
     def _():
         pass_on(1, False)
 
+    for c in range(chunks - 1):
+        spread(c)
     spread(chunks - 1)
 
     @pl.when(~inner)
     def _():
-        pass_on(2, False)
-        pass_on(3, False)
+        lon_arrived(along_z(2))
+        lon_arrived(along_z(3))
 
     for d in range(z_size):
         lon_arrived(lax.rem(z + d, z_size) * y_size + (1 - y))
@@ -215,13 +216,12 @@
 
     for copy in started:
         copy.wait_send()
-    for d in range(1, z_size):
-        pass_copies(d, False)[0].wait_send()
+    pass_copies(1, False)[0].wait_send()
 
     @pl.when(inner)
     def _():
-        for d in (1, 2):
-            pass_copies(d, True)[1].wait_send()
+        for copy in pass_copies(1, True)[1:] + pass_copies(2, True) + pass_copies(3, False):
+            copy.wait_send()
 
     share.wait_send()
     for c in range(chunks):
@@ -269,16 +269,16 @@
             pltpu.VMEM((peers, rows, width), F32),
             pltpu.VMEM((peers, block, width), F32),
             dma((chunks,)), dma((2,)), dma(()), dma((chunks,)), dma((chunks,)),
-            dma((2 * z_size,)), dma((peers,)), dma(()), dma(()),
+            dma((2 * z_size + 2,)), dma((peers,)), dma(()), dma(()),
             dma((peers,)), dma((peers,)), dma((peers,)), dma((peers,)),
         ],
         compiler_params=pltpu.CompilerParams(
-            collective_id=0, has_side_effects=True, vmem_limit_bytes=60 * 1024 * 1024
+            collective_id=0, has_side_effects=True, vmem_limit_bytes=40 * 1024 * 1024
         ),
         cost_estimate=pl.CostEstimate(
             flops=flops, bytes_accessed=4 * (field.size + longitude_matrix.size + latitude_matrix.size), transcendentals=0
         ),
-    )(field, longitude_matrix, latitude_matrix)
+    )(*[pltpu.with_memory_space_constraint(x, pltpu.HBM) for x in (field, longitude_matrix, latitude_matrix)])
 
 
 def collected(field, longitude_matrix, latitude_matrix):

time: 28.6 us -> 26.6 us (0.930)
  the two profiles are of different devices: /device:TPU:9 before, /device:TPU:1 now
where the time goes in v3:
time: 26.6 us; the launch traced here: 26.4 us
  Pallas kernels  25.7 us (97%)
  local copies, waits for them, and re-layouts  0.71 us (3%)
    pallas_call x1, Pallas kernels, exchanged(): pl.pallas_call(functools.partial(kernel, chunks, y_size), out_shape=jax.S...  25.7 us
    unnamed x1, local copies, waits for them, and re-layouts  0.71 us

profile of v3, /device:TPU:1, one launch (start us, length us, event | category | flops | bytes accessed | tf_op | source)
XLA Modules:
  0.0 26.4 jit_solution(1891239902831590330)
XLA Ops:
  0.0 25.7 %shard_map.37 = f32[8,64,128]{2,1,0:T(8,128)S(1)} custom-call(f32[8,64,1024]{2,1,0:T(8,128)} %field_hbm.1, f32[64,512]{1,0:T(8,128)} %lon_hbm.1, f32[1024,256]{1,0:T(8,128)} %lat_hbm.1), custom_call_target="tpu_custom_call" | custom-call | flops 1006632960 | bytes 3276800 | tf_op jit(solution)/shard_map/pallas_call | solution.py:253
  25.7 0.7 %copy.5 = f32[8,64,128]{2,1,0:T(8,128)} copy(f32[8,64,128]{2,1,0:T(8,128)S(1)} %shard_map.37) | data formatting | bytes 524288

commit v4 on v3

--- a/solution.py
+++ b/solution.py
@@ -23,7 +23,7 @@
 def kernel(
     chunks, y_size,
     field_hbm, lon_hbm, lat_hbm, out_ref,
-    field_buf, lat_buf, lon_buf, lat_hi, lat_lo, lon_hi, lon_lo,
+    field_buf, lat_buf, lon_buf, lat_all, lon_hi, lon_lo,
     mine, sent, got, level_buf, core_buf,
     field_sem, lat_sem, lon_sem, pair_send, pair_recv,
     lon_send, lon_recv, share_send, share_recv,
@@ -74,7 +74,6 @@
             barrier, inc=1, device_id={"lon": lax.rem(me + d, peers)}, device_id_type=pl.DeviceIdType.MESH
         )
     pl.semaphore_signal(barrier, inc=1, device_id={"lat": other}, device_id_type=pl.DeviceIdType.MESH)
-    pl.semaphore_wait(barrier, peers)
 
     def lon_copy(shard, slot, target):
         ref = lon_buf.at[shard, my_half]
@@ -85,6 +84,12 @@
     first = 1 + lax.rem(z, 2)
     second = jnp.where(lax.rem(z, 2) == 0, 2 + z // 2, z // 2)
     outward = jnp.where(z == 1, 0, 3)
+    for copy in lat_in:
+        copy.wait()
+    hi, lo = split(lat_buf[...])
+    for place, piece in enumerate((hi, lo, hi)):
+        lat_all[pl.ds(place * depth, depth)] = piece
+    pl.semaphore_wait(barrier, peers)
     lon_in.wait()
     started = [
         lon_copy(me, 0, first * y_size + y),
@@ -114,11 +119,6 @@
         for copy in pass_copies(d, outwards):
             copy.start()
 
-    for copy in lat_in:
-        copy.wait()
-    hi, lo = split(lat_buf[...])
-    lat_hi[...] = hi
-    lat_lo[...] = lo
 
     def pair_copy(c):
         span = pl.ds(c * per, per)
@@ -128,7 +128,7 @@
         field_in[c].wait()
         span = pl.ds(c * per, per)
         hi, lo = split(field_buf[span].reshape(per * rows, depth))
-        total = dot(hi, lat_hi[...]) + dot(hi, lat_lo[...]) + dot(lo, lat_hi[...])
+        total = dot(jnp.concatenate([hi, hi, lo], axis=1), lat_all[...])
         sent[span] = total[:, width:].reshape(per, rows, width)
         pair_copy(c).start()
         mine[span] = total[:, :width].reshape(per, rows, width)
@@ -259,8 +259,7 @@
             pltpu.VMEM((levels, rows, depth), F32),
             pltpu.VMEM((depth, columns), F32),
             pltpu.VMEM((peers, rows, rank), F32),
-            pltpu.VMEM((depth, columns), BF16),
-            pltpu.VMEM((depth, columns), BF16),
+            pltpu.VMEM((3 * depth, columns), BF16),
             pltpu.VMEM((rank, peers * rows), BF16),
             pltpu.VMEM((rank, peers * rows), BF16),
             pltpu.VMEM((levels, rows, width), F32),

time: 26.6 us -> 26.5 us (level)
  no operation moved by 1% of the time
where the time goes in v4:
time: 26.5 us; the launch traced here: 26.4 us
  Pallas kernels  25.7 us (97%)
  local copies, waits for them, and re-layouts  0.71 us (3%)
    pallas_call x1, Pallas kernels, exchanged(): pl.pallas_call(functools.partial(kernel, chunks, y_size), out_shape=jax.S...  25.7 us
    unnamed x1, local copies, waits for them, and re-layouts  0.71 us

profile of v4, /device:TPU:1, one launch (start us, length us, event | category | flops | bytes accessed | tf_op | source)
XLA Modules:
  0.0 26.4 jit_solution(180438789757288217)
XLA Ops:
  0.0 25.7 %shard_map.37 = f32[8,64,128]{2,1,0:T(8,128)S(1)} custom-call(f32[8,64,1024]{2,1,0:T(8,128)} %field_hbm.1, f32[64,512]{1,0:T(8,128)} %lon_hbm.1, f32[1024,256]{1,0:T(8,128)} %lat_hbm.1), custom_call_target="tpu_custom_call" | custom-call | flops 1006632960 | bytes 3276800 | tf_op jit(solution)/shard_map/pallas_call | solution.py:253
  25.7 0.7 %copy.5 = f32[8,64,128]{2,1,0:T(8,128)} copy(f32[8,64,128]{2,1,0:T(8,128)S(1)} %shard_map.37) | data formatting | bytes 524288
